TPU v7x, 768 devices: a whole 4x8x12 slice. The times are simulated.
768 devices in a mesh: dp: 32 (over y, x_lo, core), mp: 24 (over z, x_hi).
Axes of the slice: x: 4 (x_hi: 2, x_lo: 2; x = x_hi * 2 + x_lo), y: 8, z: 12, core: 2. Of those that a mesh axis runs over, the one named last changes fastest.
Arguments:
- tokens: bfloat16 [1536, 8192], P(None, 'dp'), may hold values from -6 to 6
- gate_weight: bfloat16 [8192, 15360], P('dp', 'mp'), may hold values from -0.0625 to 0.0625
- up_weight: bfloat16 [8192, 15360], P('dp', 'mp'), may hold values from -0.0625 to 0.0625
- down_weight: bfloat16 [15360, 8192], P('mp', 'dp'), may hold values from -0.046875 to 0.046875
Outputs:
- mixed: bfloat16 [1536, 8192], P('mp', 'dp')
All inputs are finite; a program needn't handle non-finite values.
Results may differ from a plain program's by a relative error of at most 0.0049.
Values may be sent and summed in bfloat16 or wider, within the bound.
A program may use at most 64 MiB of HBM per device.

v0:
```python
import jax
import jax.numpy as jnp
from jax import lax
from jax.sharding import Mesh
from jax.sharding import PartitionSpec as P

DP = ("dp_0", "dp_1", "dp_2")


def sum_in_order(tiles, axes, order):
    shape = [lax.axis_size(a) for a in axes]
    tiles = tiles.reshape(*shape, *tiles.shape[1:])
    tiles = tiles.transpose(*order, *range(len(axes), tiles.ndim))
    tiles = tiles.reshape(-1, *tiles.shape[len(axes) :])
    for k in order:
        tiles = lax.psum_scatter(tiles, axes[k], scatter_dimension=0, tiled=True)
    return tiles[0]


def split_up(value, dim, size):
    before, after = (value.shape[:dim], value.shape[dim + 1 :])
    return jnp.moveaxis(value.reshape(*before, size, -1, *after), dim, 0)


def sum_by_axis(value, axes, order, dim):
    size = lax.axis_size(axes)
    return sum_in_order(split_up(value, dim, size), axes, order)


def from_everyone(value, axis):
    size = lax.axis_size(axis)
    return lax.all_to_all(
        jnp.broadcast_to(value[None], (size, *value.shape)), axis, 0, 0, tiled=True
    )


def laid_out(tiles, dim):
    shape = list(tiles.shape[1:])
    shape[dim] *= tiles.shape[0]
    return jnp.moveaxis(tiles, 0, dim).reshape(shape)


def gathered_copies(value, axis, dim):
    tiles = from_everyone(value, axis)
    return laid_out(tiles, dim)


def sum_at_owner(value, axis, dim):
    size = lax.axis_size(axis)
    tiles = lax.all_to_all(split_up(value, dim, size), axis, 0, 0, tiled=True)
    return jnp.sum(tiles, axis=0)


def body(tokens, gate_weight, up_weight, down_weight):
    group = gate_weight.shape[1]
    both_weights = jnp.concatenate((gate_weight, up_weight), axis=1)
    summed = sum_by_axis(
        jnp.dot(tokens, both_weights, preferred_element_type=jnp.float32), DP, (2, 0, 1), 0
    )
    hidden = (jax.nn.silu(summed[:, :group]) * summed[:, group:]).astype(jnp.bfloat16)
    partial_out = jnp.dot(
        gathered_copies(hidden, DP, 0), down_weight, preferred_element_type=jnp.float32
    )
    mixed = sum_at_owner(partial_out, "mp", 0)
    return mixed.astype(jnp.bfloat16)


def solution(mesh):
    split = Mesh(mesh.devices.reshape(8, 2, 2, mesh.shape["mp"]), ("dp_0", "dp_1", "dp_2", "mp"))
    in_specs = (P(None, DP), P(DP, "mp"), P(DP, "mp"), P("mp", DP))
    out_specs = P("mp", DP)
    return jax.shard_map(body, mesh=split, in_specs=in_specs, out_specs=out_specs, check_vma=False)
```

profile of v0, /device:TPU:1, one launch (start us, length us, event | category | flops | bytes accessed | tf_op | source)
XLA Modules:
  0.0 288.2 jit_solution(16493776797020641037)
XLA Ops:
  6.5 0.0 copy-start
  6.5 0.0 reduce-scatter.4.cloned.1.call-start
  6.5 1.1 copy-done
  7.7 5.5 %convolution_bitcast_fusion = f32[1536,1280]{0,1:T(8,128)} fusion(bf16[1536,256]{1,0:T(8,128)(2,1)S(1)} %copy-done, bf16[256,640]{1,0:T(8,128)(2,1)} %param.6, bf16[256,640]{1,0:T(8,128)(2,1)} %param.5), kind=kOutput, calls=%fused_computation | convolution fusion | flops 1007943680 | bytes 9306112 | tf_op jit(solution)/shard_map/dot_general | solution.py:58
  13.1 9.1 %copy.5 = f32[1536,1280]{1,0:T(8,128)} copy(f32[1536,1280]{0,1:T(8,128)} %convolution_bitcast_fusion) | data formatting | bytes 15728640 | tf_op jit(solution)/shard_map/dot_general | solution.py:58
  22.3 7.1 %copy.6 = f32[2,8,2,48,1280]{4,3,2,1,0:T(8,128)} copy(f32[2,8,2,48,1280]{4,3,0,2,1:T(8,128)} %bitcast.14) | data formatting | bytes 15728640 | tf_op jit(solution)/shard_map/transpose | solution.py:13
  29.4 0.0 reduce-scatter.4.cloned.1.call-update
  29.4 0.0 reduce-scatter.6.cloned.1.call-start
  29.4 37.0 %reduce-scatter.4.cloned.1.call-done = f32[16,48,1280]{2,1,0:T(8,128)} async-done(((f32[32,48,1280]{2,1,0:T(8,128)}), f32[16,48,1280]{2,1,0:T(8,128)}) %reduce-scatter.4.cloned.1.call-update) | async-done | bytes 3932176 | tf_op jit(solution)/shard_map/reduce_scatter | solution.py:16
  66.4 0.0 reduce-scatter.6.cloned.1.call-update
  66.4 0.0 reduce-scatter.8.cloned.1.call-start
  66.5 60.8 %reduce-scatter.6.cloned.1.call-done = f32[2,48,1280]{2,1,0:T(8,128)} async-done(((f32[16,48,1280]{2,1,0:T(8,128)}), f32[2,48,1280]{2,1,0:T(8,128)}) %reduce-scatter.6.cloned.1.call-update) | async-done | bytes 491536 | tf_op jit(solution)/shard_map/reduce_scatter | solution.py:16
  127.2 0.0 reduce-scatter.8.cloned.1.call-update
  127.2 27.4 %reduce-scatter.8.cloned.1.call-done = f32[1,48,1280]{2,1,0:T(8,128)} async-done(((f32[2,48,1280]{2,1,0:T(8,128)}), f32[1,48,1280]{2,1,0:T(8,128)}) %reduce-scatter.8.cloned.1.call-update) | async-done | bytes 245776 | tf_op jit(solution)/shard_map/reduce_scatter | solution.py:16
  154.6 1.0 fusion.5
  155.6 0.2 broadcast_in_dim.2
  155.8 0.0 copy-start.1
  155.8 55.4 %all_to_all.10 = bf16[32,48,640]{2,1,0:T(8,128)(2,1)S(1)} all-to-all(bf16[32,48,640]{2,1,0:T(8,128)(2,1)S(1)} %broadcast_in_dim.2), channel_id=1, replica_groups=mesh['dp_0'=8,'dp_1'=2,'dp_2'=2,'mp'=24] {'dp_0','dp_1','dp_2'}, dimensions={0} | all-to-all | bytes 3932160 | tf_op jit(solution)/shard_map/all_to_all | solution.py:32
  211.2 0.0 copy-done.1
  211.2 0.8 fusion.3
  212.0 69.0 %all_to_all.11 = f32[24,64,256]{2,1,0:T(8,128)S(1)} all-to-all(f32[24,64,256]{2,1,0:T(8,128)S(1)} %fusion.3), channel_id=1, replica_groups=mesh['dp_0'=8,'dp_1'=2,'dp_2'=2,'mp'=24] {'mp'}, dimensions={0} | all-to-all | bytes 3145728 | tf_op jit(solution)/shard_map/all_to_all | solution.py:50
  281.0 0.7 reduce_sum.9
Async XLA Ops:
  6.5 1.1 copy-start
  6.5 59.9 %reduce-scatter.4.cloned.1.call-start = ((), (), s32[]{:S(2)}) async-start(), calls=%async_computation.5 | async-start | bytes 11796480 | tf_op jit(solution)/shard_map/reduce_scatter | solution.py:16
  29.4 97.8 %reduce-scatter.6.cloned.1.call-start = ((), (), s32[]{:S(2)}) async-start(), calls=%async_computation.6 | async-start | bytes 4423680 | tf_op jit(solution)/shard_map/reduce_scatter | solution.py:16
  66.4 88.2 %reduce-scatter.8.cloned.1.call-start = ((), (), s32[]{:S(2)}) async-start(), calls=%async_computation.7 | async-start | bytes 737280 | tf_op jit(solution)/shard_map/reduce_scatter | solution.py:16
  155.8 55.4 %copy-start.1 = (bf16[640,256]{1,0:T(8,128)(2,1)S(1)}, bf16[640,256]{1,0:T(8,128)(2,1)}, u32[]{:S(2)}) copy-start(bf16[640,256]{1,0:T(8,128)(2,1)} %param.7) | copy-start | bytes 983044
Sparse Core Ops, SparseCore 0:
  29.5 36.8 reduce-scatter.3
  69.9 57.3 reduce-scatter.5
  130.6 23.9 reduce-scatter.7
where the time goes:
time: 290 us; the launch traced here: 288 us
  waiting for transfers between devices  125 us (43%)
  blocking collectives  124 us (43%)
  local copies, waits for them, and re-layouts  17.5 us (6%)
  between operations  13.1 us (5%)
  matrix products  6.25 us (2%)
    reduce_scatter x3, waiting for transfers between devices, sum_in_order(): tiles = lax.psum_scatter(tiles, axes[k], scatter_dimension=0, tiled=True)  125 us
    all_to_all x1, blocking collectives, sum_at_owner(): tiles = lax.all_to_all(split_up(value, dim, size), axis, 0, 0, tiled=True)  69 us
    all_to_all x1, blocking collectives, from_everyone(): lax.all_to_all(jnp.broadcast_to(value[None], (size, *value.shape)), axis,...  55.4 us
    dot_general x1, local copies, waits for them, and re-layouts, body(): jnp.dot(tokens, both_weights, preferred_element_type=jnp.float32)  9.12 us
    transpose x1, local copies, waits for them, and re-layouts, sum_in_order(): tiles = tiles.transpose(*order, *range(len(axes), tiles.ndim))  7.11 us
  transfers between devices with their start and end apart: 3, of which 3 were waited for; matrix products, arithmetic and copies ran while one was open for 0% of the time, Pallas kernels for 0%

commit v1 on v0

v1 whole, which is shorter than its diff:
```python
import jax
import jax.numpy as jnp
from jax import lax
from jax.experimental import pallas as pl
from jax.experimental.pallas import tpu as pltpu
from jax.sharding import Mesh
from jax.sharding import PartitionSpec as P

AXES = ("y", "xl", "c", "z", "xh")
NY, NZ = 8, 12
DP = ("y", "xl", "c")
MP = ("z", "xh")
F = 640
MESH = pl.DeviceIdType.MESH
BF = jnp.bfloat16
F32 = jnp.float32


def dot(a, b):
    return jnp.dot(a, b, preferred_element_type=F32)


def hidden_kernel(
    tok, gw, uw, h_out,
    tok_b, w_b, part, s1s, s1r, s2s, s2r, s3s, s3r, s4s, s4r, xs, xr, hid,
    ex_s, ex_r, r1_s, r1_r, r2_s, r2_r, r3_s, r3_r, r4_s, r4_r, x_s, x_r,
    za_s, za_r, ya_s, ya_r, cf_s, cf_r,
):
    y, xl, c, z = (lax.axis_index(a) for a in AXES[:4])
    other_x, other_c = 1 - xl, 1 - c

    def at_y(d):
        return lax.rem(y + (d + NY), NY)

    def put(src, dst, ss, rs, **where):
        return pltpu.make_async_remote_copy(
            src_ref=src, dst_ref=dst, send_sem=ss, recv_sem=rs,
            device_id=where, device_id_type=MESH,
        )

    barrier = pltpu.get_barrier_semaphore()

    def greet(**where):
        pl.semaphore_signal(barrier, inc=1, device_id=where, device_id_type=MESH)

    greet(c=other_c)
    greet(xl=other_x)
    for d in range(1, NY):
        greet(y=at_y(d))
    for d in (1, -1):
        greet(y=at_y(d), xl=other_x)
    group = z // 3
    active = c == lax.rem(group, 2)
    from_x = group // 2
    my_first = 6 * xl + 3 * c
    for k in range(NZ):

        @pl.when(active & ((z != k) | (xl != from_x)))
        def _():
            greet(xl=from_x, z=k)

    mine = (z >= my_first) & (z < my_first + 3)
    pl.semaphore_wait(barrier, 2 + (NY - 1) + 2 + 6 - mine.astype(jnp.int32))

    exchange = [
        put(tok.at[pl.ds(6 * h + 3 * other_c, 3)], tok_b.at[h], ex_s.at[h], ex_r.at[h], c=other_c)
        for h in range(2)
    ] + [
        put(w, w_b.at[k], ex_s.at[2 + k], ex_r.at[2 + k], c=other_c)
        for k, w in enumerate((gw, uw))
    ]
    for cp in exchange:
        cp.start()
    for k, w in enumerate((gw, uw)):
        for h in range(2):
            a = tok[pl.ds(6 * h + 3 * c, 3)].reshape(384, 256)
            part[k, h] = dot(a, w[...]).reshape(3, NY, 16, F)
    for cp in exchange:
        cp.wait_recv()

    sent = list(exchange)

    def go(cp):
        cp.start()
        sent.append(cp)
        return cp

    def own(k, h, o):
        return part[k, h, :, o].reshape(48, F)

    far = at_y(4)
    for k in range(2):
        for h in range(2):
            a = tok_b[h, :, far].reshape(48, 256)
            s1s[k, h] = (own(k, h, far) + dot(a, w_b[k])).astype(BF)
    step1 = [
        go(put(s1s.at[k], s1r.at[k], r1_s.at[k], r1_r.at[k], y=at_y((-1, 1)[k]))) for k in range(2)
    ]
    for k in range(2):
        for h in range(2):
            a = tok_b[h].reshape(384, 256)
            part[k, h] = part[k, h] + dot(a, w_b[k]).reshape(3, NY, 16, F)

    step2 = [[None, None], [None, None]]

    def second(i, k):
        sign = (-1, 1)[i]
        for h in range(2):
            v = own(k, h, at_y(3 * sign))
            if i == k:
                v = v + s1r[k, h].astype(F32)
            s2s[i, k, h] = v.astype(BF)
        step2[i][k] = go(
            put(s2s.at[i, k], s2r.at[i, k], r2_s.at[i, k], r2_r.at[i, k], y=at_y(sign))
        )

    second(0, 1)
    second(1, 0)
    crossing = []
    for j in range(3):
        for k in range(2):
            xs[j, k] = own(k, other_x, at_y(j - 1)).astype(BF)
        crossing.append(go(put(xs.at[j], xr.at[j], x_s.at[j], x_r.at[j], xl=other_x)))
    for k in range(2):
        step1[k].wait_recv()
        second(k, k)

    step3 = {}
    for i, k in ((0, 1), (1, 0), (0, 0), (1, 1)):
        sign = (-1, 1)[i]
        step2[i][k].wait_recv()
        for h in range(2):
            s3s[i, k, h] = (own(k, h, at_y(2 * sign)) + s2r[i, k, h].astype(F32)).astype(BF)
        for t, where in ((0, xl), (1, other_x)):
            step3[i, k, t] = go(
                put(
                    s3s.at[i, k, where], s3r.at[i, k, t], r3_s.at[i, k, t], r3_r.at[i, k, t],
                    y=at_y(sign), xl=where,
                )
            )

    step4 = {}
    crossing[0].wait_recv()
    crossing[2].wait_recv()
    for i, k in ((0, 1), (1, 0), (0, 0), (1, 1)):
        sign = (-1, 1)[i]
        for t in range(2):
            step3[i, k, t].wait_recv()
        s4s[i, k] = (
            own(k, xl, at_y(sign))
            + s3r[i, k, 0].astype(F32)
            + s3r[i, k, 1].astype(F32)
            + xr[1 + sign, k].astype(F32)
        )
        step4[i, k] = go(
            put(s4s.at[i, k], s4r.at[i, k], r4_s.at[i, k], r4_r.at[i, k], y=at_y(sign))
        )
    crossing[1].wait_recv()
    total = []
    for k in range(2):
        for i in range(2):
            step4[i, k].wait_recv()
        total.append(own(k, xl, y) + s4r[0, k] + s4r[1, k] + xr[1, k].astype(F32))
    hid[...] = (jax.nn.silu(total[0]) * total[1]).astype(BF).reshape(3, 16, F)

    my_rows = h_out.at[pl.ds(pl.multiple_of(16 * y, 16), 16)]
    slot = my_rows.at[:, pl.ds(pl.multiple_of(z * F, 128), F)]
    for j in range(3):
        to_z = my_first + j
        same = put(hid.at[j], slot, za_s.at[j, 0], za_r, z=to_z)
        local = pltpu.make_async_copy(hid.at[j], slot, za_r)

        @pl.when(to_z != z)
        def _():
            same.start()

        @pl.when(to_z == z)
        def _():
            local.start()

        go(put(hid.at[j], slot, za_s.at[j, 1], za_r, z=to_z, xl=other_x))

    @pl.when(active)
    def _():
        pltpu.make_async_copy(my_rows, my_rows, za_r).wait()
        order = (1, 7, 2, 6, 3, 5, 4)
        outs = [put(my_rows, my_rows, ya_s.at[d], ya_r.at[d], y=at_y(d)) for d in order]
        for cp in outs:
            cp.start()
        first = put(my_rows, my_rows, cf_s.at[0], cf_r.at[0], c=other_c)
        first.start()
        forward = [first]
        for d, cp in zip(order, outs):
            rows = h_out.at[pl.ds(pl.multiple_of(16 * at_y(-d), 16), 16)]
            put(rows, rows, ya_s.at[d], ya_r.at[d], y=at_y(d)).wait_recv()
            f = put(rows, rows, cf_s.at[d], cf_r.at[d], c=other_c)
            f.start()
            forward.append(f)
        for cp in outs + forward:
            cp.wait_send()

    @pl.when(jnp.logical_not(active))
    def _():
        for d in range(NY):
            rows = h_out.at[pl.ds(pl.multiple_of(16 * at_y(-d), 16), 16)]
            put(rows, rows, cf_s.at[d], cf_r.at[d], c=other_c).wait_recv()

    for j in range(3):

        @pl.when(my_first + j != z)
        def _():
            put(hid.at[j], slot, za_s.at[j, 0], za_r, z=my_first + j).wait_send()

    for cp in sent:
        cp.wait_send()


def gathered_hidden(tokens, gate_weight, up_weight):
    dma = pltpu.SemaphoreType.DMA
    pair = [pltpu.VMEM((2, 2, 48, F), BF)] * 2
    twice = [pltpu.VMEM((2, 2, 2, 48, F), BF)] * 2
    return pl.pallas_call(
        hidden_kernel,
        out_shape=jax.ShapeDtypeStruct((16 * NY, NZ * F), BF),
        in_specs=[pl.BlockSpec(memory_space=pltpu.VMEM)] * 3,
        out_specs=pl.BlockSpec(memory_space=pltpu.VMEM),
        scratch_shapes=[
            pltpu.VMEM((2, 3, NY, 16, 256), BF),
            pltpu.VMEM((2, 256, F), BF),
            pltpu.VMEM((2, 2, 3, NY, 16, F), F32),
            *pair, *twice, *twice,
            *[pltpu.VMEM((2, 2, 48, F), F32)] * 2,
            *[pltpu.VMEM((3, 2, 48, F), BF)] * 2,
            pltpu.VMEM((3, 16, F), BF),
            *[dma((4,))] * 2, *[dma((2,))] * 2, *[dma((2, 2))] * 2,
            *[dma((2, 2, 2))] * 2, *[dma((2, 2))] * 2, *[dma((3,))] * 2,
            dma((3, 2)), dma, *[dma((NY,))] * 4,
        ],
        compiler_params=pltpu.CompilerParams(
            collective_id=0, has_side_effects=True, vmem_limit_bytes=40 << 20
        ),
        cost_estimate=pl.CostEstimate(
            flops=80_000_000_000, bytes_accessed=8_000_000, transcendentals=30720
        ),
    )(tokens.reshape(NZ, NY, 16, 256), gate_weight, up_weight)


def out_kernel(h, w, out, acc, got, ss, rs):
    xh = lax.axis_index("xh")
    barrier = pltpu.get_barrier_semaphore()
    pl.semaphore_signal(barrier, inc=1, device_id={"xh": 1 - xh}, device_id_type=MESH)
    acc[...] = dot(h[...], w[...]).reshape(2, 64, 256)
    pl.semaphore_wait(barrier, 1)
    cp = pltpu.make_async_remote_copy(
        src_ref=acc.at[1 - xh], dst_ref=got, send_sem=ss, recv_sem=rs,
        device_id={"xh": 1 - xh}, device_id_type=MESH,
    )
    cp.start()
    cp.wait()
    out[...] = (acc[xh] + got[...]).astype(BF)


def summed_out(h, w):
    dma = pltpu.SemaphoreType.DMA
    return pl.pallas_call(
        out_kernel,
        out_shape=jax.ShapeDtypeStruct((64, 256), BF),
        in_specs=[pl.BlockSpec(memory_space=pltpu.VMEM)] * 2,
        out_specs=pl.BlockSpec(memory_space=pltpu.VMEM),
        scratch_shapes=[
            pltpu.VMEM((2, 64, 256), F32), pltpu.VMEM((64, 256), F32), dma, dma,
        ],
        compiler_params=pltpu.CompilerParams(
            collective_id=1, has_side_effects=True, vmem_limit_bytes=24 << 20
        ),
    )(h, w)


def body(tokens, gate_weight, up_weight, down_weight):
    down = lax.all_gather(down_weight, "z", axis=0, tiled=True)
    hidden = gathered_hidden(tokens, gate_weight, up_weight)
    return summed_out(hidden, down)


def solution(mesh):
    split = Mesh(mesh.devices.reshape(NY, 2, 2, NZ, 2), AXES)
    in_specs = (P(None, DP), P(DP, MP), P(DP, MP), P(MP, DP))
    return jax.shard_map(body, mesh=split, in_specs=in_specs, out_specs=P(MP, DP), check_vma=False)
```

time: 290 us -> 106 us (0.37)
  the two profiles are of different devices: /device:TPU:1 before, /device:TPU:138 now
where the time goes in v1:
time: 106 us
  Pallas kernels  86 us (81%)
  between operations  13.4 us (13%)
  local copies, waits for them, and re-layouts  5.79 us (5%)
    pallas_call x1, Pallas kernels, gathered_hidden(): pl.pallas_call(hidden_kernel, out_shape=jax.ShapeDtypeStruct((16 * NY, NZ...  79.3 us
    pallas_call x1, Pallas kernels, summed_out(): pl.pallas_call(out_kernel, out_shape=jax.ShapeDtypeStruct((64, 256), BF),...  6.63 us
    unnamed x9, local copies, waits for them, and re-layouts  5.79 us
  transfers between devices with their start and end apart: 1, of which 0 were waited for; matrix products, arithmetic and copies ran while one was open for 0% of the time, Pallas kernels for 75%

profile of v1, /device:TPU:138, one launch (start us, length us, event | category | flops | bytes accessed | tf_op | source)
XLA Modules:
  0.0 105.9 jit_solution(12607508097232278008)
XLA Ops:
  6.5 0.0 all-gather.2.cloned.1.call-start
  6.5 0.7 all-gather.2.cloned.1.call-update
  7.3 0.0 copy-start.1
  7.3 1.1 %copy-done.1 = bf16[1536,256]{1,0:T(8,128)(2,1)S(1)} copy-done((bf16[1536,256]{1,0:T(8,128)(2,1)S(1)}, bf16[1536,256]{1,0:T(8,128)(2,1)}, u32[]{:S(2)}) %copy-start.1) | copy-done | bytes 786456
  8.4 0.0 copy-start.2
  8.4 1.0 copy-done.2
  9.4 0.0 copy-start.3
  9.4 1.0 copy-done.3
  10.3 79.3 %shard_map.46.h = bf16[128,7680]{1,0:T(8,128)(2,1)S(1)} custom-call(bf16[12,8,16,256]{3,2,1,0:T(8,128)(2,1)S(1)} %bitcast.1, bf16[256,640]{1,0:T(8,128)(2,1)S(1)} %copy-done.2, bf16[256,640]{1,0:T(8,128)(2,1)S(1)} %copy-done.3), custom_call_target="tpu_custom_call" | custom-call | flops 80000000000 | bytes 8000000 | tf_op jit(solution)/shard_map/pallas_call | solution.py:222
  89.7 0.0 all-gather.2.cloned.1.call-done.w
  89.7 0.0 copy-start
  89.7 2.1 %copy-done = bf16[7680,256]{1,0:T(8,128)(2,1)S(1)} copy-done((bf16[7680,256]{1,0:T(8,128)(2,1)S(1)}, bf16[7680,256]{1,0:T(8,128)(2,1)}, u32[]{:S(2)}) %copy-start) | copy-done | bytes 3932184
  91.8 6.6 %shard_map.47 = bf16[64,256]{1,0:T(8,128)(2,1)S(1)} custom-call(bf16[128,7680]{1,0:T(8,128)(2,1)S(1)} %shard_map.46.h, bf16[7680,256]{1,0:T(8,128)(2,1)S(1)} %copy-done), custom_call_target="tpu_custom_call" | custom-call | tf_op jit(solution)/shard_map/pallas_call | solution.py:265
  98.5 0.6 copy.6
Async XLA Ops:
  6.5 83.2 %all-gather.2.cloned.1.call-start = ((), (), s32[]{:S(2)}) async-start(), calls=%async_computation | async-start | bytes 4259840 | tf_op jit(solution)/shard_map/all_gather | solution.py:280
  7.3 1.1 %copy-start.1 = (bf16[1536,256]{1,0:T(8,128)(2,1)S(1)}, bf16[1536,256]{1,0:T(8,128)(2,1)}, u32[]{:S(2)}) copy-start(bf16[1536,256]{1,0:T(8,128)(2,1)} %param.4) | copy-start | bytes 2359300
  8.4 1.0 copy-start.2
  9.4 1.0 copy-start.3
  89.7 2.1 %copy-start = (bf16[7680,256]{1,0:T(8,128)(2,1)S(1)}, bf16[7680,256]{1,0:T(8,128)(2,1)}, u32[]{:S(2)}) copy-start(bf16[7680,256]{1,0:T(8,128)(2,1)} %all-gather.2.cloned.1.call-done.w) | copy-start | bytes 11796484
Sparse Core Ops, SparseCore 0:
  9.7 76.5 all-gather.1

commit v2 on v1

v2 whole, which is shorter than its diff:
```python
import jax
import jax.numpy as jnp
from jax import lax
from jax.experimental import pallas as pl
from jax.experimental.pallas import tpu as pltpu
from jax.sharding import Mesh
from jax.sharding import PartitionSpec as P

AXES = ("y", "xl", "c", "z", "xh")
NY, NZ = 8, 12
DP = ("y", "xl", "c")
MP = ("z", "xh")
F = 640
MESH = pl.DeviceIdType.MESH
BF = jnp.bfloat16
F32 = jnp.float32


def dot(a, b):
    return jnp.dot(a, b, preferred_element_type=F32)


def block_kernel(
    tok_in, gw_in, uw_in, wd_in, out,
    tok, w_a, tok_b, w_b, part, s1s, s1r, s2s, s2r, s3s, s3r, s4s, s4r, xs, xr, hid,
    hall, down, acc, got,
    in_s, ex_s, ex_r, r1_s, r1_r, r2_s, r2_r, r3_s, r3_r, r4_s, r4_r, x_s, x_r,
    za_s, za_r, ya_s, ya_r, xa_s, xa_r, cf_s, cf_r, zr_s, zr_r, xh_s, xh_r,
):
    y, xl, c, z, xh = (lax.axis_index(a) for a in AXES)
    other_x, other_c = 1 - xl, 1 - c

    def at_y(d):
        return lax.rem(y + (d + NY), NY)

    def at_z(d):
        return lax.rem(z + (d + NZ), NZ)

    def put(src, dst, ss, rs, **where):
        return pltpu.make_async_remote_copy(
            src_ref=src, dst_ref=dst, send_sem=ss, recv_sem=rs,
            device_id=where, device_id_type=MESH,
        )

    barrier = pltpu.get_barrier_semaphore()

    def greet(**where):
        pl.semaphore_signal(barrier, inc=1, device_id=where, device_id_type=MESH)

    greet(c=other_c)
    greet(xl=other_x)
    greet(xh=1 - xh)
    for d in range(1, NY):
        greet(y=at_y(d))
    for d in (1, -1):
        greet(y=at_y(d), xl=other_x)
        greet(z=at_z(d))
    group = z // 3
    active = c == lax.rem(group, 2)
    for k in range(6):

        @pl.when(active & (z != 6 * xl + k))
        def _():
            greet(xl=group // 2, z=6 * xl + k)

    loads = [
        pltpu.make_async_copy(src, dst, in_s.at[k])
        for k, (src, dst) in enumerate(
            ((gw_in, w_a.at[0]), (uw_in, w_a.at[1]), (tok_in, tok), (wd_in, down.at[z]))
        )
    ]
    for cp in loads:
        cp.start()
    for cp in loads:
        cp.wait()
    my_first = 6 * xl + 3 * c
    mine = (z >= my_first) & (z < my_first + 3)
    pl.semaphore_wait(barrier, 3 + (NY - 1) + 4 + 3 - mine.astype(jnp.int32))

    def ring(i, h, k):
        sign = (1, -1)[i]
        block = down.at[at_z(-sign * (k - 1)), pl.ds(320 * h, 320)]
        return put(block, block, zr_s.at[i, h, k], zr_r.at[i, h, k], z=at_z(sign))

    def last(i, h):
        return 6 if i == h else 5

    def advance(k, chunks=(0, 1)):
        for h in chunks:
            for i in range(2):
                if k <= last(i, h):
                    sign = (1, -1)[i]
                    block = down.at[at_z(-sign * k), pl.ds(320 * h, 320)]
                    put(block, block, zr_s.at[i, h, k], zr_r.at[i, h, k], z=at_z(sign)).wait_recv()
                if k < last(i, h):
                    ring(i, h, k + 1).start()

    exchange = [
        put(tok.at[pl.ds(6 * h + 3 * other_c, 3)], tok_b.at[h], ex_s.at[h], ex_r.at[h], c=other_c)
        for h in range(2)
    ] + [
        put(w_a.at[k], w_b.at[k], ex_s.at[2 + k], ex_r.at[2 + k], c=other_c)
        for k in range(2)
    ]
    for cp in exchange:
        cp.start()
    for h in range(2):
        for i in range(2):
            ring(i, h, 1).start()
    for k in range(2):
        for h in range(2):
            a = tok[pl.ds(6 * h + 3 * c, 3)].reshape(384, 256)
            part[k, h] = dot(a, w_a[k]).reshape(3, NY, 16, F)
    for cp in exchange:
        cp.wait_recv()

    sent = list(exchange)

    def go(cp):
        cp.start()
        sent.append(cp)
        return cp

    def own(k, h, o):
        return part[k, h, :, o].reshape(48, F)

    far = at_y(4)
    for k in range(2):
        for h in range(2):
            a = tok_b[h, :, far].reshape(48, 256)
            s1s[k, h] = (own(k, h, far) + dot(a, w_b[k])).astype(BF)
    step1 = [
        go(put(s1s.at[k], s1r.at[k], r1_s.at[k], r1_r.at[k], y=at_y((-1, 1)[k]))) for k in range(2)
    ]
    for k in range(2):
        for h in range(2):
            a = tok_b[h].reshape(384, 256)
            part[k, h] = part[k, h] + dot(a, w_b[k]).reshape(3, NY, 16, F)

    step2 = [[None, None], [None, None]]

    def second(i, k):
        sign = (-1, 1)[i]
        for h in range(2):
            v = own(k, h, at_y(3 * sign))
            if i == k:
                v = v + s1r[k, h].astype(F32)
            s2s[i, k, h] = v.astype(BF)
        step2[i][k] = go(
            put(s2s.at[i, k], s2r.at[i, k], r2_s.at[i, k], r2_r.at[i, k], y=at_y(sign))
        )

    second(0, 1)
    second(1, 0)
    crossing = []
    for j in range(3):
        for k in range(2):
            xs[j, k] = own(k, other_x, at_y(j - 1)).astype(BF)
        crossing.append(go(put(xs.at[j], xr.at[j], x_s.at[j], x_r.at[j], xl=other_x)))
    for k in range(2):
        step1[k].wait_recv()
        second(k, k)

    advance(1)

    step3 = {}
    for i, k in ((0, 1), (1, 0), (0, 0), (1, 1)):
        sign = (-1, 1)[i]
        step2[i][k].wait_recv()
        for h in range(2):
            s3s[i, k, h] = (own(k, h, at_y(2 * sign)) + s2r[i, k, h].astype(F32)).astype(BF)
        for t, where in ((0, xl), (1, other_x)):
            step3[i, k, t] = go(
                put(
                    s3s.at[i, k, where], s3r.at[i, k, t], r3_s.at[i, k, t], r3_r.at[i, k, t],
                    y=at_y(sign), xl=where,
                )
            )

    advance(2)

    step4 = {}
    crossing[0].wait_recv()
    crossing[2].wait_recv()
    for i, k in ((0, 1), (1, 0), (0, 0), (1, 1)):
        sign = (-1, 1)[i]
        for t in range(2):
            step3[i, k, t].wait_recv()
        s4s[i, k] = (
            own(k, xl, at_y(sign))
            + s3r[i, k, 0].astype(F32)
            + s3r[i, k, 1].astype(F32)
            + xr[1 + sign, k].astype(F32)
        )
        step4[i, k] = go(
            put(s4s.at[i, k], s4r.at[i, k], r4_s.at[i, k], r4_r.at[i, k], y=at_y(sign))
        )
    advance(3)
    crossing[1].wait_recv()
    total = []
    for k in range(2):
        for i in range(2):
            step4[i, k].wait_recv()
        total.append(own(k, xl, y) + s4r[0, k] + s4r[1, k] + xr[1, k].astype(F32))
    hid[...] = (jax.nn.silu(total[0]) * total[1]).astype(BF).reshape(3, 16, F)

    def piece(d, x):
        row = pl.multiple_of(16 * at_y(-d), 16)
        return hall.at[pl.ds(row, 16), pl.ds(pl.multiple_of(6 * F * x, 128), 6 * F)]

    to_x = z // 6
    row = pl.multiple_of(16 * y, 16)
    slot = hall.at[pl.ds(row, 16), pl.ds(pl.multiple_of(z * F, 128), F)]

    def along_z(j):
        return put(hid.at[j], slot, za_s.at[j], za_r, z=my_first + j, xl=to_x)

    for j in range(3):

        @pl.when(my_first + j != z)
        def _():
            along_z(j).start()

        @pl.when(my_first + j == z)
        def _():
            pltpu.make_async_copy(hid.at[j], slot, za_r).start()

    advance(4)

    order = (1, 7, 2, 6, 3, 5, 4)

    def along_y(d):
        own_piece = piece(0, xl)
        return put(own_piece, own_piece, ya_s.at[d], ya_r.at[d], y=at_y(d))

    def across(d):
        return put(piece(d, xl), piece(d, xl), xa_s.at[d], xa_r.at[d], xl=other_x)

    def to_core(d, t):
        p = piece(d, xl if t == 0 else other_x)
        return put(p, p, cf_s.at[t, d], cf_r.at[t, d], c=other_c)

    @pl.when(active)
    def _():
        pltpu.make_async_copy(piece(0, xl), piece(0, xl), za_r).wait()
        for d in order:
            along_y(d).start()
        across(0).start()
        to_core(0, 0).start()

    advance(5)

    def came_across(d):
        p = piece(d, other_x)
        put(p, p, xa_s.at[d], xa_r.at[d], xl=other_x).wait_recv()
        to_core(d, 1).start()

    @pl.when(active)
    def _():
        late = (0, *order)
        for n, d in enumerate(order):
            p = piece(d, xl)
            put(p, p, ya_s.at[d], ya_r.at[d], y=at_y(d)).wait_recv()
            across(d).start()
            to_core(d, 0).start()
            if n >= 2:
                came_across(late[n - 2])
        for d in late[5:]:
            came_across(d)

    @pl.when(jnp.logical_not(active))
    def _():
        for d in (0, *order):
            for t in range(2):
                to_core(d, t).wait_recv()

    advance(6)

    def rows_of(t):
        lhs = hall[pl.ds(pl.multiple_of(64 * t, 64), 64), :]
        return dot(lhs, down[...].reshape(NZ * F, 256))

    acc[...] = rows_of(1 - xh)
    final = put(acc, got, xh_s, xh_r, xh=1 - xh)
    final.start()
    result = rows_of(xh)
    final.wait_recv()
    out[...] = (result + got[...]).astype(BF)

    final.wait_send()
    for j in range(3):

        @pl.when(my_first + j != z)
        def _():
            along_z(j).wait_send()

    @pl.when(active)
    def _():
        for d in order:
            along_y(d).wait_send()
        for d in (0, *order):
            across(d).wait_send()
            for t in range(2):
                to_core(d, t).wait_send()

    for h in range(2):
        for i in range(2):
            for k in range(1, last(i, h) + 1):
                ring(i, h, k).wait_send()
    for cp in sent:
        cp.wait_send()


def body(tokens, gate_weight, up_weight, down_weight):
    dma = pltpu.SemaphoreType.DMA
    twice = [pltpu.VMEM((2, 2, 2, 48, F), BF)] * 2
    return pl.pallas_call(
        block_kernel,
        out_shape=jax.ShapeDtypeStruct((64, 256), BF),
        in_specs=[pl.BlockSpec(memory_space=pl.ANY)] * 4,
        out_specs=pl.BlockSpec(memory_space=pltpu.VMEM),
        scratch_shapes=[
            pltpu.VMEM((NZ, NY, 16, 256), BF),
            pltpu.VMEM((2, 256, F), BF),
            pltpu.VMEM((2, 3, NY, 16, 256), BF),
            pltpu.VMEM((2, 256, F), BF),
            pltpu.VMEM((2, 2, 3, NY, 16, F), F32),
            *[pltpu.VMEM((2, 2, 48, F), BF)] * 2, *twice, *twice,
            *[pltpu.VMEM((2, 2, 48, F), F32)] * 2,
            *[pltpu.VMEM((3, 2, 48, F), BF)] * 2,
            pltpu.VMEM((3, 16, F), BF),
            pltpu.VMEM((16 * NY, NZ * F), BF),
            pltpu.VMEM((NZ, F, 256), BF),
            *[pltpu.VMEM((64, 256), F32)] * 2,
            dma((4,)),
            *[dma((4,))] * 2, *[dma((2,))] * 2, *[dma((2, 2))] * 2,
            *[dma((2, 2, 2))] * 2, *[dma((2, 2))] * 2, *[dma((3,))] * 2,
            dma((3,)), dma, *[dma((NY,))] * 4, *[dma((2, NY))] * 2,
            *[dma((2, 2, 7))] * 2, dma, dma,
        ],
        compiler_params=pltpu.CompilerParams(
            collective_id=0, has_side_effects=True, vmem_limit_bytes=60 << 20
        ),
    )(tokens.reshape(NZ, NY, 16, 256), gate_weight, up_weight, down_weight)


def solution(mesh):
    split = Mesh(mesh.devices.reshape(NY, 2, 2, NZ, 2), AXES)
    in_specs = (P(None, DP), P(DP, MP), P(DP, MP), P(MP, DP))
    return jax.shard_map(body, mesh=split, in_specs=in_specs, out_specs=P(MP, DP), check_vma=False)
```

time: 106 us -> 85.5 us (0.81)
  the two profiles are of different devices: /device:TPU:138 before, /device:TPU:17 now
where the time goes in v2:
time: 85.5 us; the launch traced here: 85.3 us
  Pallas kernels  83.9 us (98%)
  local copies, waits for them, and re-layouts  1.38 us (2%)
    pallas_call x1, Pallas kernels, body(): pl.pallas_call(block_kernel, out_shape=jax.ShapeDtypeStruct((64, 256), BF...  83.9 us

profile of v2, /device:TPU:17, one launch (start us, length us, event | category | flops | bytes accessed | tf_op | source)
XLA Modules:
  0.0 85.3 jit_solution(8689434671737500558)
XLA Ops:
  0.0 83.9 %shard_map.46 = bf16[64,256]{1,0:T(8,128)(2,1)} custom-call(bf16[12,8,16,256]{3,2,1,0:T(8,128)(2,1)} %bitcast.1, bf16[256,640]{1,0:T(8,128)(2,1)} %gw_in.1, bf16[256,640]{1,0:T(8,128)(2,1)} %uw_in.1, bf16[640,256]{1,0:T(8,128)(2,1)} %wd_in.1), custom_call_target="tpu_custom_call" | custom-call | tf_op jit(solution)/shard_map/pallas_call | solution.py:317
  83.9 1.4 %copy.6 = bf16[64,256]{1,0:T(8,128)(2,1)} copy(bf16[64,256]{1,0:T(8,128)(2,1)} %shard_map.46) | data formatting | bytes 65536

commit v3 on v2

v3 whole, which is shorter than its diff:
```python
import jax
import jax.numpy as jnp
from jax import lax
from jax.experimental import pallas as pl
from jax.experimental.pallas import tpu as pltpu
from jax.sharding import Mesh
from jax.sharding import PartitionSpec as P

AXES = ("y", "xl", "c", "z", "xh")
NY, NZ = 8, 12
WHEN = {
    ('third', 0): ((1, 0),),
    ('third', 1): ((1, 1),),
    ('fourth', 0): ((2, 0),),
    ('fourth', 1): ((2, 1),),
    ('hidden', 0): ((3, 0),),
    ('hidden', 1): ((3, 1),),
    ('gather', 0): ((4, 0),),
    ('gather', 1): ((4, 1),),
    ('pass', 4): ((5, 0),),
    ('pass', 7): ((5, 1),),
    ('last', 0): ((6, 0), (6, 1)),
}
DP = ("y", "xl", "c")
MP = ("z", "xh")
F = 640
CHUNKS = ((0, 256), (256, 384))
MESH = pl.DeviceIdType.MESH
BF = jnp.bfloat16
F32 = jnp.float32


def dot(a, b):
    return jnp.dot(a, b, preferred_element_type=F32)


def block_kernel(
    tok_in, gw_in, uw_in, wd_in, out,
    tok, w_a, tok_b, w_b, part, xs, xr, down, acc, got, ring_bufs,
    in_s, ex_s, ex_r, r1_s, r1_r, r2_s, r2_r, r3_s, r3_r, r4_s, r4_r, x_s, x_r,
    za_s, za_r, ya_s, ya_r, xa_s, xa_r, cf_s, cf_r, zr_s, zr_r, xh_s, xh_r,
):
    y, xl, c, z, xh = (lax.axis_index(a) for a in AXES)
    other_x, other_c = 1 - xl, 1 - c

    def at_y(d):
        return lax.rem(y + (d + NY), NY)

    def at_z(d):
        return lax.rem(z + (d + NZ), NZ)

    def put(src, dst, ss, rs, **where):
        return pltpu.make_async_remote_copy(
            src_ref=src, dst_ref=dst, send_sem=ss, recv_sem=rs,
            device_id=where, device_id_type=MESH,
        )

    barrier = pltpu.get_barrier_semaphore()

    def greet(**where):
        pl.semaphore_signal(barrier, inc=1, device_id=where, device_id_type=MESH)

    greet(c=other_c)
    greet(xl=other_x)
    greet(xh=1 - xh)
    for d in range(1, NY):
        greet(y=at_y(d))
    for d in (1, -1):
        greet(y=at_y(d), xl=other_x)
        greet(z=at_z(d))
    group = z // 3
    active = c == lax.rem(group, 2)
    for k in range(6):

        @pl.when(active & (z != 6 * xl + k))
        def _():
            greet(xl=group // 2, z=6 * xl + k)

    loads = [
        pltpu.make_async_copy(src, dst, in_s.at[k])
        for k, (src, dst) in enumerate(
            ((gw_in, w_a.at[0]), (uw_in, w_a.at[1]), (tok_in, tok), (wd_in, down.at[z]))
        )
    ]
    for cp in loads:
        cp.start()
    for cp in loads:
        cp.wait()
    my_first = 6 * xl + 3 * c
    mine = (z >= my_first) & (z < my_first + 3)
    pl.semaphore_wait(barrier, 3 + (NY - 1) + 4 + 3 - mine.astype(jnp.int32))

    def ring(i, h, k):
        sign = (1, -1)[i]
        block = down.at[at_z(-sign * (k - 1)), pl.ds(320 * h, 320)]
        return put(block, block, zr_s.at[i, h, k], zr_r.at[i, h, k], z=at_z(sign))

    def last(i, h):
        return 6 if i == h else 5

    def advance(k, h):
        for i in range(2):
            if k <= last(i, h):
                sign = (1, -1)[i]
                block = down.at[at_z(-sign * k), pl.ds(320 * h, 320)]
                put(block, block, zr_s.at[i, h, k], zr_r.at[i, h, k], z=at_z(sign)).wait_recv()
            if k < last(i, h):
                ring(i, h, k + 1).start()

    def onward(stage, n):
        for k, h in WHEN.get((stage, n), ()):
            advance(k, h)

    exchange = [
        put(tok.at[pl.ds(6 * h + 3 * other_c, 3)], tok_b.at[h], ex_s.at[h], ex_r.at[h], c=other_c)
        for h in range(2)
    ] + [
        put(w_a.at[k], w_b.at[k], ex_s.at[2 + k], ex_r.at[2 + k], c=other_c)
        for k in range(2)
    ]
    for cp in exchange:
        cp.start()
    for h in range(2):
        for i in range(2):
            ring(i, h, 1).start()
    for k in range(2):
        for h in range(2):
            a = tok[pl.ds(6 * h + 3 * c, 3)].reshape(384, 256)
            part[k, h] = dot(a, w_a[k]).reshape(3, NY, 16, F)
    for cp in exchange:
        cp.wait_recv()

    sent = list(exchange)

    def go(cp):
        cp.start()
        sent.append(cp)
        return cp

    def own(k, h, o):
        return part[k, h, :, o].reshape(48, F)

    def cols(n):
        return pl.ds(CHUNKS[n][0], CHUNKS[n][1])

    def own_cols(k, h, o, n):
        return part[k, h, :, o, :, cols(n)].reshape(48, CHUNKS[n][1])

    def bufs(n):
        return ring_bufs[n]

    def long_way(n):
        return n % 2

    step1, step2, step3, step4 = {}, {}, {}, {}
    many = range(len(CHUNKS))
    far = at_y(4)
    for n in many:
        s1s, s1r = bufs(n)[0:2]
        for k in range(2):
            for h in range(2):
                a = tok_b[h, :, far].reshape(48, 256)
                s1s[h, k] = (own_cols(k, h, far, n) + dot(a, w_b[k, :, cols(n)])).astype(BF)
        step1[n] = go(
            put(s1s, s1r, r1_s.at[n], r1_r.at[n], y=at_y((-1, 1)[long_way(n)]))
        )
    for k in range(2):
        for h in range(2):
            a = tok_b[h].reshape(384, 256)
            part[k, h] = part[k, h] + dot(a, w_b[k]).reshape(3, NY, 16, F)

    def second(n, i):
        s1r, s2s, s2r = bufs(n)[1:4]
        sign = (-1, 1)[i]
        for k in range(2):
            for h in range(2):
                v = own_cols(k, h, at_y(3 * sign), n)
                if i == long_way(n):
                    v = v + s1r[h, k].astype(F32)
                s2s[i, h, k] = v.astype(BF)
        step2[n, i] = go(
            put(s2s.at[i], s2r.at[i], r2_s.at[n, i], r2_r.at[n, i], y=at_y(sign))
        )

    for n in many:
        second(n, 1 - long_way(n))
    crossing = []
    for j in range(3):
        for k in range(2):
            xs[j, k] = own(k, other_x, at_y(j - 1)).astype(BF)
        crossing.append(go(put(xs.at[j], xr.at[j], x_s.at[j], x_r.at[j], xl=other_x)))
    for n in many:
        step1[n].wait_recv()
        second(n, long_way(n))
        onward('second', n)

    def third(n, i):
        s2r, s3s, s3r = bufs(n)[3:6]
        sign = (-1, 1)[i]
        step2[n, i].wait_recv()
        for k in range(2):
            for h in range(2):
                s3s[i, h, k] = (
                    own_cols(k, h, at_y(2 * sign), n) + s2r[i, h, k].astype(F32)
                ).astype(BF)
        for t, where in ((0, xl), (1, other_x)):
            step3[n, i, t] = go(
                put(
                    s3s.at[i, where], s3r.at[i, t], r3_s.at[n, i, t], r3_r.at[n, i, t],
                    y=at_y(sign), xl=where,
                )
            )

    for n in many:
        third(n, 1 - long_way(n))
        third(n, long_way(n))
        onward('third', n)

    crossing[0].wait_recv()
    crossing[2].wait_recv()

    def fourth(n, i):
        s3r, s4s, s4r = bufs(n)[5:8]
        sign = (-1, 1)[i]
        for t in range(2):
            step3[n, i, t].wait_recv()
        for k in range(2):
            s4s[i, k] = (
                own_cols(k, xl, at_y(sign), n)
                + s3r[i, 0, k].astype(F32)
                + s3r[i, 1, k].astype(F32)
                + xr[1 + sign, k, :, cols(n)].astype(F32)
            )
        step4[n, i] = go(
            put(s4s.at[i], s4r.at[i], r4_s.at[n, i], r4_r.at[n, i], y=at_y(sign))
        )

    for n in many:
        fourth(n, 1 - long_way(n))
        fourth(n, long_way(n))
        onward('fourth', n)
    crossing[1].wait_recv()

    to_x = z // 6
    row = pl.multiple_of(16 * y, 16)

    def slot(n):
        w = CHUNKS[n][1]
        return bufs(n)[9].at[pl.ds(row, 16), pl.ds(pl.multiple_of(z * w, 128), w)]

    def along_z(n, j):
        return put(
            bufs(n)[8].at[j], slot(n), za_s.at[n, j], za_r.at[n], z=my_first + j, xl=to_x
        )

    for n in many:
        s4r, hid = bufs(n)[7:9]
        for i in range(2):
            step4[n, i].wait_recv()
        gate, up = (
            own_cols(k, xl, y, n) + s4r[0, k] + s4r[1, k] + xr[1, k, :, cols(n)].astype(F32)
            for k in range(2)
        )
        hid[...] = (jax.nn.silu(gate) * up).astype(BF).reshape(hid.shape)
        for j in range(3):

            @pl.when(my_first + j != z)
            def _():
                along_z(n, j).start()

            @pl.when(my_first + j == z)
            def _():
                pltpu.make_async_copy(hid.at[j], slot(n), za_r.at[n]).start()

        onward('hidden', n)


    order = (1, 7, 2, 6, 3, 5, 4)

    def piece(n, d, x):
        start = pl.multiple_of(16 * at_y(-d), 16)
        w = 6 * CHUNKS[n][1]
        return bufs(n)[9].at[pl.ds(start, 16), pl.ds(pl.multiple_of(w * x, 128), w)]

    def along_y(n, d):
        p = piece(n, 0, xl)
        return put(p, p, ya_s.at[n, d], ya_r.at[n, d], y=at_y(d))

    def across(n, d):
        p = piece(n, d, xl)
        return put(p, p, xa_s.at[n, d], xa_r.at[n, d], xl=other_x)

    def to_core(n, d, t):
        p = piece(n, d, xl if t == 0 else other_x)
        return put(p, p, cf_s.at[n, t, d], cf_r.at[n, t, d], c=other_c)

    for n in many:

        @pl.when(active)
        def _():
            p = piece(n, 0, xl)
            pltpu.make_async_copy(p, p, za_r.at[n]).wait()
            for d in order:
                along_y(n, d).start()
            across(n, 0).start()
            to_core(n, 0, 0).start()

        onward('gather', n)

    def came_along(n, d):
        p = piece(n, d, xl)
        put(p, p, ya_s.at[n, d], ya_r.at[n, d], y=at_y(d)).wait_recv()
        across(n, d).start()
        to_core(n, d, 0).start()

    def came_across(n, d):
        p = piece(n, d, other_x)
        put(p, p, xa_s.at[n, d], xa_r.at[n, d], xl=other_x).wait_recv()
        to_core(n, d, 1).start()

    events = [(n, d) for n in many for d in order]
    crossed = [(n, d) for n in many for d in (0, *order)]

    def order_of(d):
        return (0, *order).index(d) - 1

    @pl.when(active)
    def _():
        done = 0
        for count, (n, d) in enumerate(events):
            came_along(n, d)
            while done < len(crossed) and crossed[done][0] * 7 + order_of(crossed[done][1]) + 4 < count:
                came_across(*crossed[done])
                done += 1
            onward('pass', count)
        for at in crossed[done:]:
            came_across(*at)

    @pl.when(jnp.logical_not(active))
    def _():
        for count, (n, d) in enumerate(crossed):
            for t in range(2):
                to_core(n, d, t).wait_recv()
            onward('pass', count)

    onward('last', 0)

    def rows_of(t):
        r = pl.ds(pl.multiple_of(64 * t, 64), 64)
        return sum(
            dot(bufs(n)[9][r, :], down[:, cols(n), :].reshape(NZ * CHUNKS[n][1], 256))
            for n in many
        )

    acc[...] = rows_of(1 - xh)
    final = put(acc, got, xh_s, xh_r, xh=1 - xh)
    final.start()
    result = rows_of(xh)
    final.wait_recv()
    out[...] = (result + got[...]).astype(BF)

    final.wait_send()
    for n in many:
        for j in range(3):

            @pl.when(my_first + j != z)
            def _():
                along_z(n, j).wait_send()

    @pl.when(active)
    def _():
        for n in many:
            for d in order:
                along_y(n, d).wait_send()
            for d in (0, *order):
                across(n, d).wait_send()
                for t in range(2):
                    to_core(n, d, t).wait_send()

    for h in range(2):
        for i in range(2):
            for k in range(1, last(i, h) + 1):
                ring(i, h, k).wait_send()
    for cp in sent:
        cp.wait_send()


def body(tokens, gate_weight, up_weight, down_weight):
    dma = pltpu.SemaphoreType.DMA
    m = len(CHUNKS)

    def chunk_bufs(w):
        return [
            *[pltpu.VMEM((2, 2, 48, w), BF)] * 2,
            *[pltpu.VMEM((2, 2, 2, 48, w), BF)] * 4,
            *[pltpu.VMEM((2, 2, 48, w), F32)] * 2,
            pltpu.VMEM((3, 16, w), BF),
            pltpu.VMEM((16 * NY, NZ * w), BF),
        ]

    return pl.pallas_call(
        block_kernel,
        out_shape=jax.ShapeDtypeStruct((64, 256), BF),
        in_specs=[pl.BlockSpec(memory_space=pltpu.HBM)] * 4,
        out_specs=pl.BlockSpec(memory_space=pltpu.VMEM),
        scratch_shapes=[
            pltpu.VMEM((NZ, NY, 16, 256), BF),
            pltpu.VMEM((2, 256, F), BF),
            pltpu.VMEM((2, 3, NY, 16, 256), BF),
            pltpu.VMEM((2, 256, F), BF),
            pltpu.VMEM((2, 2, 3, NY, 16, F), F32),
            *[pltpu.VMEM((3, 2, 48, F), BF)] * 2,
            pltpu.VMEM((NZ, F, 256), BF),
            *[pltpu.VMEM((64, 256), F32)] * 2,
            [chunk_bufs(w) for _, w in CHUNKS],
            dma((4,)),
            *[dma((4,))] * 2, *[dma((m,))] * 2, *[dma((m, 2))] * 2,
            *[dma((m, 2, 2))] * 2, *[dma((m, 2))] * 2, *[dma((3,))] * 2,
            dma((m, 3)), dma((m,)), *[dma((m, NY))] * 4, *[dma((m, 2, NY))] * 2,
            *[dma((2, 2, 7))] * 2, dma, dma,
        ],
        compiler_params=pltpu.CompilerParams(
            collective_id=0, has_side_effects=True, vmem_limit_bytes=55040 << 10
        ),
    )(tokens.reshape(NZ, NY, 16, 256), gate_weight, up_weight, down_weight)


def solution(mesh):
    split = Mesh(mesh.devices.reshape(NY, 2, 2, NZ, 2), AXES)
    in_specs = (P(None, DP), P(DP, MP), P(DP, MP), P(MP, DP))
    return jax.shard_map(body, mesh=split, in_specs=in_specs, out_specs=P(MP, DP), check_vma=False)
```

time: 85.5 us -> 80.9 us (0.946)
  the two profiles are of different devices: /device:TPU:17 before, /device:TPU:1 now
where the time goes in v3:
time: 80.9 us; the launch traced here: 80 us
  Pallas kernels  79.4 us (98%)
    pallas_call x1, Pallas kernels, body(): pl.pallas_call(block_kernel, out_shape=jax.ShapeDtypeStruct((64, 256), BF...  79.4 us

profile of v3, /device:TPU:1, one launch (start us, length us, event | category | flops | bytes accessed | tf_op | source)
XLA Modules:
  0.0 80.0 jit_solution(988293375259265997)
XLA Ops:
  0.0 79.4 %shard_map.46 = bf16[64,256]{1,0:T(8,128)(2,1)S(1)} custom-call(bf16[12,8,16,256]{3,2,1,0:T(8,128)(2,1)} %bitcast.1, bf16[256,640]{1,0:T(8,128)(2,1)} %gw_in.1, bf16[256,640]{1,0:T(8,128)(2,1)} %uw_in.1, bf16[640,256]{1,0:T(8,128)(2,1)} %wd_in.1), custom_call_target="tpu_custom_call" | custom-call | tf_op jit(solution)/shard_map/pallas_call | solution.py:401
  79.4 0.6 copy.6

commit v4 on v3

--- a/solution.py
+++ b/solution.py
@@ -9,17 +9,18 @@
 AXES = ("y", "xl", "c", "z", "xh")
 NY, NZ = 8, 12
 WHEN = {
-    ('third', 0): ((1, 0),),
-    ('third', 1): ((1, 1),),
-    ('fourth', 0): ((2, 0),),
-    ('fourth', 1): ((2, 1),),
-    ('hidden', 0): ((3, 0),),
-    ('hidden', 1): ((3, 1),),
-    ('gather', 0): ((4, 0),),
-    ('gather', 1): ((4, 1),),
-    ('pass', 4): ((5, 0),),
-    ('pass', 7): ((5, 1),),
-    ('last', 0): ((6, 0), (6, 1)),
+    ('second', 1): ((1, 0),),
+    ('third', 0): ((1, 1),),
+    ('third', 1): ((2, 0),),
+    ('fourth', 0): ((2, 1),),
+    ('fourth', 1): ((3, 0),),
+    ('hidden', 0): ((3, 1),),
+    ('hidden', 1): ((4, 0),),
+    ('gather', 0): ((4, 1),),
+    ('pass', 1): ((5, 0),),
+    ('pass', 5): ((5, 1),),
+    ('pass', 9): ((6, 0),),
+    ('last', 0): ((6, 1),),
 }
 DP = ("y", "xl", "c")
 MP = ("z", "xh")

time: 80.9 us -> 79.5 us (0.983)
  no operation moved by 1% of the time
where the time goes in v4:
time: 79.5 us; the launch traced here: 79.3 us
  Pallas kernels  78.7 us (99%)
    pallas_call x1, Pallas kernels, body(): pl.pallas_call(block_kernel, out_shape=jax.ShapeDtypeStruct((64, 256), BF...  78.7 us

profile of v4, /device:TPU:1, one launch (start us, length us, event | category | flops | bytes accessed | tf_op | source)
XLA Modules:
  0.0 79.3 jit_solution(5627821653465680469)
XLA Ops:
  0.0 78.7 %shard_map.46 = bf16[64,256]{1,0:T(8,128)(2,1)S(1)} custom-call(bf16[12,8,16,256]{3,2,1,0:T(8,128)(2,1)} %bitcast.1, bf16[256,640]{1,0:T(8,128)(2,1)} %gw_in.1, bf16[256,640]{1,0:T(8,128)(2,1)} %uw_in.1, bf16[640,256]{1,0:T(8,128)(2,1)} %wd_in.1), custom_call_target="tpu_custom_call" | custom-call | tf_op jit(solution)/shard_map/pallas_call | solution.py:402
  78.7 0.6 copy.6

commit v5 on v4

--- a/solution.py
+++ b/solution.py
@@ -301,16 +301,23 @@
         def _():
             p = piece(n, 0, xl)
             pltpu.make_async_copy(p, p, za_r.at[n]).wait()
-            for d in order:
+            for d in order[:-1]:
                 along_y(n, d).start()
             across(n, 0).start()
             to_core(n, 0, 0).start()
 
         onward('gather', n)
 
+    def passed_on(n):
+        d, sign = ((3, 1), (5, -1))[n % 2]
+        p = piece(n, d, xl)
+        return put(p, p, ya_s.at[n, 4], ya_r.at[n, 4], y=at_y(sign))
+
     def came_along(n, d):
         p = piece(n, d, xl)
         put(p, p, ya_s.at[n, d], ya_r.at[n, d], y=at_y(d)).wait_recv()
+        if d == (3, 5)[n % 2]:
+            passed_on(n).start()
         across(n, d).start()
         to_core(n, d, 0).start()
 
@@ -371,8 +378,9 @@
     @pl.when(active)
     def _():
         for n in many:
-            for d in order:
+            for d in order[:-1]:
                 along_y(n, d).wait_send()
+            passed_on(n).wait_send()
             for d in (0, *order):
                 across(n, d).wait_send()
                 for t in range(2):

time: 79.5 us -> 82.9 us (1.043)
  Pallas kernels: 78.7 us -> 82.1 us
    pallas_call x1, Pallas kernels: 78.7 us -> 82.1 us  [body(): pl.pallas_call(block_kernel, out_shape=jax.ShapeDtypeStruct((64, 256), BF...]
where the time goes in v5:
time: 82.9 us; the launch traced here: 82.7 us
  Pallas kernels  82.1 us (99%)
    pallas_call x1, Pallas kernels, body(): pl.pallas_call(block_kernel, out_shape=jax.ShapeDtypeStruct((64, 256), BF...  82.1 us

profile of v5, /device:TPU:1, one launch (start us, length us, event | category | flops | bytes accessed | tf_op | source)
XLA Modules:
  0.0 82.7 jit_solution(1121748981217759319)
XLA Ops:
  0.0 82.1 %shard_map.46 = bf16[64,256]{1,0:T(8,128)(2,1)S(1)} custom-call(bf16[12,8,16,256]{3,2,1,0:T(8,128)(2,1)} %bitcast.1, bf16[256,640]{1,0:T(8,128)(2,1)} %gw_in.1, bf16[256,640]{1,0:T(8,128)(2,1)} %uw_in.1, bf16[640,256]{1,0:T(8,128)(2,1)} %wd_in.1), custom_call_target="tpu_custom_call" | custom-call | tf_op jit(solution)/shard_map/pallas_call | solution.py:410
  82.1 0.6 copy.6
